TPU v7x, 32 devices: a whole 2x2x4 slice. The times are simulated.
32 devices in a mesh: groups: 2 (over y), mem: 8 (over z, x), lat: 2 (over core).
Axes of the slice: x: 2, y: 2, z: 4, core: 2. Of those that a mesh axis runs over, the one named last changes fastest.
Arguments:
- ensemble: float32 [16, 6, 256, 512], P(('groups', 'mem'), None, 'lat'), parts along dimension 0, may hold values from -1.5 to 1.5
- forcing_table: float32 [8, 256, 512], P(None, 'lat'), may hold values from -3 to 3
- ancestors: int32 [16], P('groups'), parts along dimension 0, may hold values from 0 to 7
- selector: int32 [16], P(('groups', 'mem')), parts along dimension 0, may hold values from 0 to 7
Outputs:
- advanced: float32 [16, 6, 256, 512], P(('groups', 'mem'), None, 'lat'), parts along dimension 0
There are 2 independent parts, one for each index of `groups`. A program takes and returns all parts, laid end to end along the dimension named above; an argument that names none is the same for every part. Nothing has to cross between parts.
Inputs may be any that keep to these rules, and one draw needn't show every extreme that they name: `ancestors`: index of a member of the same ensemble; some parents are named by several slots, many by none. `selector`: index of a forcing pattern.
All inputs are finite; a program needn't handle non-finite values.
Results may differ from a plain program's by a relative error of at most 0.00002.
Values sent between devices are 32-bit elements; how exact they have to be, the bound alone decides.
A program may use at most 192 MiB of HBM per device.

v0:
```python
import jax
import jax.numpy as jnp
from jax import lax
from jax.sharding import PartitionSpec as P

STEPS = 3


TIME_STEP = 0.25
DENSITY_RATIO = 0.9
DRAG_RATE = 0.1
CORIOLIS_MEAN = 0.5


def padded(block, sides, width):
    for axis, dim in sides:
        count = lax.axis_size(axis)
        forward = [(i, i + 1) for i in range(count - 1)]
        backward = [(target, source) for source, target in forward]
        low = lax.ppermute(
            lax.slice_in_dim(block, block.shape[dim] - width, None, axis=dim), axis, forward
        )
        high = lax.ppermute(lax.slice_in_dim(block, 0, width, axis=dim), axis, backward)
        block = jnp.concatenate([low, block, high], axis=dim)
    return block


def row_below(values):
    widths = [(0, 0)] * (values.ndim - 2) + [(1, 0), (0, 0)]
    return jnp.pad(values[..., :-1, :], widths)


def row_above(values):
    widths = [(0, 0)] * (values.ndim - 2) + [(0, 1), (0, 0)]
    return jnp.pad(values[..., 1:, :], widths)


def col_west(values):
    return jnp.roll(values, 1, axis=-1)


def col_east(values):
    return jnp.roll(values, -1, axis=-1)


def advance(fields, forcing, row_ids, total):
    inside = ((row_ids >= 0.0) & (row_ids < total)).astype(jnp.float32)[:, None]
    wall_mask = ((row_ids >= 1.0) & (row_ids < total)).astype(jnp.float32)[:, None]
    coriolis_u = CORIOLIS_MEAN + (row_ids / total - 0.5)[:, None]
    coriolis_v = CORIOLIS_MEAN + ((row_ids - 0.5) / total - 0.5)[:, None]
    heights = []
    zonal = []
    merid = []
    for layer_index in range(2):
        height = fields[:, 3 * layer_index]
        speed_u = fields[:, 3 * layer_index + 1]
        speed_v = fields[:, 3 * layer_index + 2] * wall_mask
        thickness = 1.0 + height
        flux_x = speed_u * (0.5 * (thickness + col_west(thickness)))
        flux_y = speed_v * (0.5 * (thickness + row_below(thickness)))
        divergence = col_east(flux_x) - flux_x + (row_above(flux_y) - flux_y)
        heights.append(height - TIME_STEP * divergence)
        zonal.append(speed_u)
        merid.append(speed_v)
    pressures = [heights[0] + heights[1], DENSITY_RATIO * heights[0] + heights[1]]
    outputs = []
    for layer_index in range(2):
        speed_u = zonal[layer_index]
        speed_v = merid[layer_index]
        pressure = pressures[layer_index]
        extra = forcing if layer_index == 0 else -DRAG_RATE * speed_u
        above_v = row_above(speed_v)
        mean_v = 0.25 * (speed_v + col_west(speed_v) + above_v + col_west(above_v))
        new_u = speed_u + TIME_STEP * (
            coriolis_u * mean_v - (pressure - col_west(pressure)) + extra
        )
        below_u = row_below(speed_u)
        mean_u = 0.25 * (speed_u + col_east(speed_u) + below_u + col_east(below_u))
        new_v = (
            speed_v + TIME_STEP * (-coriolis_v * mean_u - (pressure - row_below(pressure)))
        ) * wall_mask
        outputs.extend([heights[layer_index] * inside, new_u * inside, new_v * inside])
    return jnp.stack(outputs, axis=1)


def copy_members(block, ancestors):
    slots, fields_count, band_rows, columns = block.shape
    flat = block.reshape(slots, fields_count, band_rows * columns)
    taken = jnp.take(
        lax.all_to_all(flat, "mem", split_axis=2, concat_axis=0, tiled=True), ancestors, axis=0
    )
    moved = lax.all_to_all(taken, "mem", split_axis=0, concat_axis=2, tiled=True)
    return moved.reshape(slots, fields_count, band_rows, columns)


def pick_forcing(table, selector):
    patterns = jnp.arange(table.shape[0], dtype=jnp.int32)
    chosen = selector[:, None, None, None] == patterns[None, :, None, None]
    return jnp.sum(jnp.where(chosen, table[None], jnp.float32(0.0)), axis=1)


def on_device(ensemble, forcing_table, ancestors, selector):
    slots, fields_count, band_rows, columns = ensemble.shape
    total = jnp.float32(band_rows * lax.axis_size("lat"))
    base_row = (lax.axis_index("lat") * band_rows).astype(jnp.float32)
    margin = 2 * STEPS
    parents = copy_members(ensemble, ancestors)
    slot_forcing = pick_forcing(forcing_table, selector)
    row_ids = base_row - margin + jnp.arange(band_rows + 2 * margin).astype(jnp.float32)
    combined = jnp.concatenate([parents, slot_forcing[:, None]], axis=1)
    extended = padded(combined, (("lat", 2),), margin)
    fields = extended[:, :fields_count]
    wide_forcing = extended[:, fields_count]
    for step_index in range(STEPS):
        fields = advance(fields, wide_forcing, row_ids, total)
    return fields[:, :, margin:-margin]


def solution(mesh):
    placed = (
        P(("groups", "mem"), None, "lat", None),
        P(None, "lat", None),
        P("groups"),
        P(("groups", "mem")),
    )
    return jax.shard_map(
        on_device,
        mesh=mesh,
        in_specs=placed,
        out_specs=P(("groups", "mem"), None, "lat", None),
        check_vma=False,
    )
```

profile of v0, /device:TPU:0, one launch (start us, length us, event | category | flops | bytes accessed | tf_op | source)
XLA Modules:
  0.0 556.4 jit_solution(10381373765545520294)
XLA Ops:
  0.0 17.9 %copy.16 = f32[1,6,128,512]{1,3,2,0:T(8,128)} copy(f32[1,6,128,512]{3,2,1,0:T(8,128)} %param.4) | data formatting | bytes 3145728 | tf_op jit(solution)/shard_map/reshape | solution.py:88
  17.9 0.6 broadcast.413
  18.5 291.0 %reduce.2 = f32[65536,6]{1,0:T(8,128)} reduce(f32[65536,1,6]{2,1,0:T(1,128)} %bitcast.133, f32[]{:T(128)} %broadcast.413), dimensions={1}, to_apply=%bitcast.84.reduce_sub_computation | reduce | bytes 3145732
  309.4 33.8 %reshape.545 = f32[8,1,49152]{2,1,0:T(1,128)} reshape(f32[65536,6]{1,0:T(8,128)} %reduce.2) | data formatting | bytes 3145728
  343.3 7.6 %all-to-all-start = ((f32[8,1,49152]{2,1,0:T(1,128)}), f32[8,1,49152]{2,1,0:T(1,128)S(1)}, u32[]{:S(2)}, u32[]{:S(2)}) async-start(f32[8,1,49152]{2,1,0:T(1,128)} %reshape.545), calls=%async_computation | async-start | bytes 3145728 | tf_op jit(solution)/shard_map/all_to_all | solution.py:90
  350.9 36.8 %all-to-all-done = f32[8,1,49152]{2,1,0:T(1,128)S(1)} async-done(((f32[8,1,49152]{2,1,0:T(1,128)}), f32[8,1,49152]{2,1,0:T(1,128)S(1)}, u32[]{:S(2)}, u32[]{:S(2)}) %all-to-all-start) | async-done | bytes 1572896 | tf_op jit(solution)/shard_map/all_to_all | solution.py:90
  387.6 4.4 reduce.3
  392.0 66.7 %reshape.546 = f32[65536,1,6]{2,1,0:T(1,128)} reshape(f32[8,49152]{1,0:T(8,128)S(1)} %reduce.3) | data formatting | bytes 3145728
  458.7 18.4 %copy.14 = f32[1,6,8,8192]{3,1,2,0:T(8,128)S(1)} copy(f32[1,6,8,8192]{1,3,2,0:T(8,128)} %bitcast.134) | data formatting | bytes 3145728 | tf_op jit(solution)/shard_map/all_to_all | solution.py:90
  477.2 2.0 gather_fusion
  479.2 3.2 broadcast_select_fusion
  482.3 3.6 all-to-all-start.1
  486.7 1.9 select_reduce_fusion
  488.6 45.8 %all-to-all-done.1 = f32[8,6,8192]{2,1,0:T(8,128)S(1)} async-done(((f32[8,6,8192]{2,1,0:T(8,128)}), f32[8,6,8192]{2,1,0:T(8,128)S(1)}, u32[]{:S(2)}, u32[]{:S(2)}) %all-to-all-start.1) | async-done | bytes 1572896 | tf_op jit(solution)/shard_map/all_to_all | solution.py:92
  534.4 2.1 copy.15
  536.4 1.6 reshape.535
  538.0 1.3 collective-permute-start
  539.3 1.3 collective-permute-start.1
  540.7 1.9 collective-permute-done.1
  542.6 0.3 pad_maximum_fusion
  543.1 0.4 fusion.3
  544.6 0.5 fusion.51
  545.9 0.3 multiply_multiply_fusion.2
  546.7 0.5 fusion.21
  547.9 0.3 multiply_multiply_fusion.3
  548.8 0.4 fusion.160
  549.4 0.5 fusion.65
  550.9 0.3 multiply_multiply_fusion.1
  551.7 0.3 multiply_multiply_fusion
  553.2 0.4 fusion.87
  554.0 0.4 fusion.129
  554.6 1.3 slice.606
  (101 shorter events, 7.0 us)
Async XLA Ops:
  343.3 7.6 %copy-start = (s32[8]{0:T(128)S(1)}, s32[8]{0:T(128)}, u32[]{:S(2)}) copy-start(s32[8]{0:T(128)} %param.6) | copy-start | bytes 100
  343.3 44.4 %all-to-all-start = ((f32[8,1,49152]{2,1,0:T(1,128)}), f32[8,1,49152]{2,1,0:T(1,128)S(1)}, u32[]{:S(2)}, u32[]{:S(2)}) async-start(f32[8,1,49152]{2,1,0:T(1,128)} %reshape.545), calls=%async_computation | async-start | bytes 3145728 | tf_op jit(solution)/shard_map/all_to_all | solution.py:90
  482.3 52.1 %all-to-all-start.1 = ((f32[8,6,8192]{2,1,0:T(8,128)}), f32[8,6,8192]{2,1,0:T(8,128)S(1)}, u32[]{:S(2)}, u32[]{:S(2)}) async-start(f32[8,6,8192]{2,1,0:T(8,128)} %broadcast_select_fusion), calls=%async_computation.1 | async-start | bytes 4194304 | tf_op jit(solution)/shard_map/all_to_all | solution.py:92
  538.0 2.6 collective-permute-start
  539.3 3.2 collective-permute-start.1
where the time goes:
time: 565 us; the launch traced here: 556 us
  other arithmetic  307 us (54%)
  local copies, waits for them, and re-layouts  150 us (27%)
  waiting for transfers between devices  84.5 us (15%)
  starting transfers between devices  13.8 us (2%)
    unnamed x6, other arithmetic  292 us
    unnamed x5, local copies, waits for them, and re-layouts  101 us
    all_to_all x1, waiting for transfers between devices, copy_members(): lax.all_to_all(taken, 'mem', split_axis=0, concat_axis=2, tiled=True)  45.8 us
    all_to_all x1, waiting for transfers between devices, copy_members(): lax.all_to_all(flat, 'mem', split_axis=2, concat_axis=0, tiled=True)  36.8 us
    all_to_all x1, local copies, waits for them, and re-layouts, copy_members(): lax.all_to_all(flat, 'mem', split_axis=2, concat_axis=0, tiled=True)  18.4 us
    reshape x1, local copies, waits for them, and re-layouts, copy_members(): flat = block.reshape(slots, fields_count, band_rows * columns)  17.9 us
  transfers between devices with their start and end apart: 4, of which 3 were waited for; matrix products, arithmetic and copies ran while one was open for 0% of the time, Pallas kernels for 0%

commit v1 on v0

v1 whole, which is shorter than its diff:
```python
import functools

import jax
import jax.numpy as jnp
from jax import lax
from jax.experimental import pallas as pl
from jax.experimental.pallas import tpu as pltpu
from jax.sharding import PartitionSpec as P

STEPS = 3
TIME_STEP = 0.25
DENSITY_RATIO = 0.9
DRAG_RATE = 0.1
CORIOLIS_MEAN = 0.5
HALO = 8
CHUNK = 8


def col_west(values):
    return pltpu.roll(values, 1, axis=1)


def col_east(values):
    return pltpu.roll(values, values.shape[1] - 1, axis=1)


def window_kernel(lat_count, selector, parents, low, high, table, out, state, other, forcing, sems):
    band_rows, columns = parents.shape[1:]
    first = 2 * HALO
    end = first + band_rows
    copies = [
        (parents, state.at[:, pl.ds(first, band_rows)]),
        (low.at[pl.ds(0, 6)], state.at[:, pl.ds(HALO, HALO)]),
        (high.at[pl.ds(0, 6)], state.at[:, pl.ds(end, HALO)]),
        (table.at[selector[0]], forcing.at[pl.ds(first, band_rows)]),
        (low.at[6], forcing.at[pl.ds(HALO, HALO)]),
        (high.at[6], forcing.at[pl.ds(end, HALO)]),
    ]
    copies = [pltpu.make_async_copy(src, dst, sems.at[i]) for i, (src, dst) in enumerate(copies)]
    for copy in copies:
        copy.start()
    for copy in copies:
        copy.wait()

    lat = lax.axis_index("lat")
    base_row = lat * band_rows
    total = band_rows * lat_count
    tile_rows = lax.broadcasted_iota(jnp.int32, (CHUNK, 128), 0)

    def spread(values):
        return jnp.concatenate([values] * (columns // 128), axis=1)

    wide_rows = lax.broadcasted_iota(jnp.int32, (CHUNK, columns), 0)
    is_first, is_last = wide_rows == 0, wide_rows == CHUNK - 1

    for field in (2, 5):
        walled = spread((base_row + tile_rows >= 1).astype(jnp.float32))
        state[field, first : first + CHUNK, :] *= walled

    def advance(src, dst, start):
        def at(ref, field, shift=0):
            return ref[field, pl.ds(pl.multiple_of(start + shift, CHUNK), CHUNK), :]

        def below(here, ref, field):
            return pltpu.roll(jnp.where(is_last, at(ref, field, -CHUNK), here), 1, axis=0)

        def above(here, ref, field):
            return pltpu.roll(jnp.where(is_first, at(ref, field, CHUNK), here), CHUNK - 1, axis=0)

        rows_int = base_row + (start - first) + tile_rows
        rows = rows_int.astype(jnp.float32)
        wall = spread(((rows_int >= 1) & (rows_int < total)).astype(jnp.float32))
        coriolis_u = spread(CORIOLIS_MEAN + (rows / total - 0.5))
        coriolis_v = spread(CORIOLIS_MEAN + ((rows - 0.5) / total - 0.5))
        layers = []
        for field in (0, 3):
            height, speed_u, speed_v = at(src, field), at(src, field + 1), at(src, field + 2)
            above_v = above(speed_v, src, field + 2)
            thickness = 1.0 + height
            flux_x = speed_u * (0.5 * (thickness + col_west(thickness)))
            flux_y = speed_v * (0.5 * (thickness + (1.0 + below(height, src, field))))
            flux_y_above = above_v * (0.5 * ((1.0 + above(height, src, field)) + thickness))
            divergence = (col_east(flux_x) - flux_x) + (flux_y_above - flux_y)
            new_height = height - TIME_STEP * divergence
            dst[field, pl.ds(start, CHUNK), :] = new_height
            layers.append((new_height, speed_u, speed_v, above_v))
        upper, lower = layers[0][0], layers[1][0]
        upper_below, lower_below = below(upper, dst, 0), below(lower, dst, 3)
        pressures = [upper + lower, DENSITY_RATIO * upper + lower]
        pressures_below = [upper_below + lower_below, DENSITY_RATIO * upper_below + lower_below]
        for layer, field in enumerate((0, 3)):
            _, speed_u, speed_v, above_v = layers[layer]
            pressure = pressures[layer]
            if layer == 0:
                extra = forcing[pl.ds(start, CHUNK), :]
            else:
                extra = -DRAG_RATE * speed_u
            sum_v = speed_v + above_v
            mean_v = 0.25 * (sum_v + col_west(sum_v))
            new_u = speed_u + TIME_STEP * (
                coriolis_u * mean_v - (pressure - col_west(pressure)) + extra
            )
            sum_u = speed_u + below(speed_u, src, field + 1)
            mean_u = 0.25 * (sum_u + col_east(sum_u))
            new_v = speed_v + TIME_STEP * (
                -coriolis_v * mean_u - (pressure - pressures_below[layer])
            )
            dst[field + 1, pl.ds(start, CHUNK), :] = new_u
            dst[field + 2, pl.ds(start, CHUNK), :] = new_v * wall

    src, dst = state, other
    for step in range(STEPS):
        def body(index, carry, src=src, dst=dst):
            advance(src, dst, pl.multiple_of(HALO + index * CHUNK, CHUNK))
            return carry

        lax.fori_loop(0, (band_rows + 2 * HALO) // CHUNK, body, 0)
        src, dst = dst, src
    done = pltpu.make_async_copy(src.at[:, pl.ds(first, band_rows)], out, sems.at[0])
    done.start()
    done.wait()


def run_window(parents, low, high, table, selector, lat_count):
    fields_count, band_rows, columns = parents.shape
    held = (fields_count, band_rows + 4 * HALO, columns)
    return pl.pallas_call(
        functools.partial(window_kernel, lat_count),
        out_shape=jax.ShapeDtypeStruct(parents.shape, jnp.float32),
        in_specs=[pl.BlockSpec(memory_space=pltpu.SMEM)] + [pl.BlockSpec(memory_space=pl.ANY)] * 4,
        out_specs=pl.BlockSpec(memory_space=pl.ANY),
        scratch_shapes=[
            pltpu.VMEM(held, jnp.float32),
            pltpu.VMEM(held, jnp.float32),
            pltpu.VMEM(held[1:], jnp.float32),
            pltpu.SemaphoreType.DMA((6,)),
        ],
        compiler_params=pltpu.CompilerParams(vmem_limit_bytes=24 * 1024 * 1024),
        name="window",
    )(selector, parents, low, high, table)


def copy_members(block, ancestors):
    pieces = lax.all_to_all(block, "mem", split_axis=2, concat_axis=0, tiled=True)
    taken = jnp.take(pieces, ancestors, axis=0)
    return lax.all_to_all(taken, "mem", split_axis=0, concat_axis=2, tiled=True)[0]


def edge_rows(values):
    count = lax.axis_size("lat")
    forward = [(i, i + 1) for i in range(count - 1)]
    backward = [(target, source) for source, target in forward]
    low = lax.ppermute(values[:, -HALO:], "lat", forward)
    high = lax.ppermute(values[:, :HALO], "lat", backward)
    return low, high


def on_device(ensemble, forcing_table, ancestors, selector):
    parents = copy_members(ensemble, ancestors)
    table_edges = jnp.concatenate([forcing_table[:, :HALO], forcing_table[:, -HALO:]], axis=1)
    chosen = lax.dynamic_index_in_dim(table_edges, selector[0], 0)
    ends = jnp.concatenate([parents[:, :HALO], parents[:, -HALO:]], axis=1)
    low, high = edge_rows(jnp.concatenate([ends, chosen], axis=0))
    return run_window(parents, low, high, forcing_table, selector, lax.axis_size("lat"))[None]


def solution(mesh):
    placed = (
        P(("groups", "mem"), None, "lat", None),
        P(None, "lat", None),
        P("groups"),
        P(("groups", "mem")),
    )
    return jax.shard_map(
        on_device,
        mesh=mesh,
        in_specs=placed,
        out_specs=P(("groups", "mem"), None, "lat", None),
        check_vma=False,
    )
```

time: 565 us -> 127 us (0.22); the launches traced: 556 us -> 126 us
  other arithmetic: 307 us -> 1.44 us
  local copies, waits for them, and re-layouts: 150 us -> 9.45 us
  Pallas kernels: 0 us -> 14.1 us
    unnamed x6 -> x0, other arithmetic: 292 us -> none
    unnamed x5, local copies, waits for them, and re-layouts: 101 us -> 3.69 us
    reshape x2 -> x0, local copies, waits for them, and re-layouts: 19.5 us -> none  [the longest x1 17.9 us: copy_members(): flat = block.reshape(slots, fields_count, band_rows * columns)]
    all_to_all x2, local copies, waits for them, and re-layouts: 20.5 us -> 3.65 us  [the longest x1 2.04 us: copy_members(): lax.all_to_all(block, 'mem', split_axis=2, concat_axis=0, tiled=True)]
    pallas_call x0 -> x1, Pallas kernels: none -> 14.1 us  [run_window(): pl.pallas_call(functools.partial(window_kernel, lat_count), out_shape=jax...]
    slice x79 -> x3, local copies, waits for them, and re-layouts: 6.49 us -> 0.05 us  [the longest x1 0.02 us: on_device(): forcing_table[:, -HALO:]]
where the time goes in v1:
time: 127 us; the launch traced here: 126 us
  waiting for transfers between devices  86 us (68%)
  starting transfers between devices  14.4 us (11%)
  Pallas kernels  14.1 us (11%)
  local copies, waits for them, and re-layouts  9.45 us (7%)
  other arithmetic  1.44 us (1%)
    all_to_all x1, waiting for transfers between devices, copy_members(): lax.all_to_all(block, 'mem', split_axis=2, concat_axis=0, tiled=True)  48.2 us
    all_to_all x1, waiting for transfers between devices, copy_members(): lax.all_to_all(taken, 'mem', split_axis=0, concat_axis=2, tiled=True)[0]  35.9 us
    pallas_call x1, Pallas kernels, run_window(): pl.pallas_call(functools.partial(window_kernel, lat_count), out_shape=jax...  14.1 us
    all_to_all x1, starting transfers between devices, copy_members(): lax.all_to_all(block, 'mem', split_axis=2, concat_axis=0, tiled=True)  7.38 us
    all_to_all x1, starting transfers between devices, copy_members(): lax.all_to_all(taken, 'mem', split_axis=0, concat_axis=2, tiled=True)[0]  4.42 us
    unnamed x5, local copies, waits for them, and re-layouts  3.69 us
  transfers between devices with their start and end apart: 4, of which 3 were waited for; matrix products, arithmetic and copies ran while one was open for 0% of the time, Pallas kernels for 0%

profile of v1, /device:TPU:0, one launch (start us, length us, event | category | flops | bytes accessed | tf_op | source)
XLA Modules:
  0.0 126.2 jit_solution(7044146635780606315)
XLA Ops:
  0.0 3.7 %copy.8 = f32[1,6,128,512]{3,1,0,2:T(8,128)} copy(f32[1,6,128,512]{3,2,1,0:T(8,128)} %param.4) | data formatting | bytes 3145728 | tf_op args[0]
  3.7 0.0 copy-start.1
  3.7 7.4 %all-to-all-start = ((f32[1,6,128,512]{3,1,0,2:T(8,128)}), f32[1,6,128,512]{3,1,0,2:T(8,128)S(1)}, u32[]{:S(2)}, u32[]{:S(2)}) async-start(f32[1,6,128,512]{3,1,0,2:T(8,128)} %copy.8), calls=%async_computation | async-start | bytes 4194304 | tf_op jit(solution)/shard_map/all_to_all | solution.py:144
  11.1 0.0 copy-done.1
  11.1 48.2 %all-to-all-done = f32[1,6,128,512]{3,1,0,2:T(8,128)S(1)} async-done(((f32[1,6,128,512]{3,1,0,2:T(8,128)}), f32[1,6,128,512]{3,1,0,2:T(8,128)S(1)}, u32[]{:S(2)}, u32[]{:S(2)}) %all-to-all-start) | async-done | bytes 1572896 | tf_op jit(solution)/shard_map/all_to_all | solution.py:144
  59.3 2.0 %copy.15 = f32[1,6,8,16,512]{4,3,1,2,0:T(8,128)} copy(f32[1,6,8,16,512]{4,1,3,2,0:T(8,128)S(1)} %bitcast.17) | data formatting | bytes 3145728 | tf_op jit(solution)/shard_map/all_to_all | solution.py:144
  61.4 2.1 %gather_fusion = f32[8,6,16,512]{3,2,1,0:T(8,128)S(1)} fusion(f32[8,6,16,512]{3,2,1,0:T(8,128)} %bitcast.18, s32[1024]{0:T(1024)S(1)} %pad_clamp_fusion), kind=kCustom, calls=%fused_computation | custom fusion | bytes 3145760 | tf_op jit(solution)/shard_map/jit(_take)/gather | solution.py:145
  63.4 1.4 %broadcast_select_fusion = f32[8,6,16,512]{3,2,1,0:T(8,128)} fusion(f32[8,6,16,512]{3,2,1,0:T(8,128)S(1)} %gather_fusion, pred[8]{0:T(512)(128)(4,1)S(1)} %compare_and_fusion), kind=kLoop, calls=%fused_computation.2 | loop fusion | flops 393216 | bytes 3145736 | tf_op jit(solution)/shard_map/jit(_take)/select_n | solution.py:145
  64.8 0.0 copy-start
  64.8 4.4 %all-to-all-start.1 = ((f32[8,6,16,512]{3,2,1,0:T(8,128)}), f32[8,6,16,512]{3,2,1,0:T(8,128)}, u32[]{:S(2)}, u32[]{:S(2)}) async-start(f32[8,6,16,512]{3,2,1,0:T(8,128)} %broadcast_select_fusion), calls=%async_computation.1 | async-start | bytes 3145728 | tf_op jit(solution)/shard_map/all_to_all | solution.py:146
  69.9 0.0 copy-done
  70.0 35.9 %all-to-all-done.1 = f32[8,6,16,512]{3,2,1,0:T(8,128)} async-done(((f32[8,6,16,512]{3,2,1,0:T(8,128)}), f32[8,6,16,512]{3,2,1,0:T(8,128)}, u32[]{:S(2)}, u32[]{:S(2)}) %all-to-all-start.1) | async-done | bytes 1572896 | tf_op jit(solution)/shard_map/all_to_all | solution.py:146
  105.9 1.6 %copy.11 = f32[1,6,8,16,512]{4,3,2,1,0:T(8,128)S(1)} copy(f32[1,6,8,16,512]{4,3,1,2,0:T(8,128)} %bitcast.4) | data formatting | bytes 3145728 | tf_op jit(solution)/shard_map/all_to_all | solution.py:146
  107.6 1.3 %collective-permute-start = (f32[7,8,512]{2,1,0:T(8,128)S(1)}, f32[7,8,512]{2,1,0:T(8,128)S(1)}, u32[]{:S(2)}, u32[]{:S(2)}) collective-permute-start(f32[7,8,512]{2,1,0:T(8,128)S(1)} %get-tuple-element.10), channel_id=1, source_target_pairs={{0,1},{2,3},{4,5},{6,7},{8,9},{10,11},{12,13},{14,15},{16,17},{18,... | collective-permute-start | bytes 344072 | tf_op jit(solution)/shard_map/ppermute | solution.py:153
  108.9 1.3 %collective-permute-start.1 = (f32[7,8,512]{2,1,0:T(8,128)S(1)}, f32[7,8,512]{2,1,0:T(8,128)S(1)}, u32[]{:S(2)}, u32[]{:S(2)}) collective-permute-start(f32[7,8,512]{2,1,0:T(8,128)S(1)} %get-tuple-element.9), channel_id=1, source_target_pairs={{1,0},{3,2},{5,4},{7,6},{9,8},{11,10},{13,12},{15,14},{17,16},{19,... | collective-permute-start | bytes 344072 | tf_op jit(solution)/shard_map/ppermute | solution.py:154
  110.2 0.0 collective-permute-done.low
  110.2 1.9 %collective-permute-done.1.high = f32[7,8,512]{2,1,0:T(8,128)S(1)} collective-permute-done((f32[7,8,512]{2,1,0:T(8,128)S(1)}, f32[7,8,512]{2,1,0:T(8,128)S(1)}, u32[]{:S(2)}, u32[]{:S(2)}) %collective-permute-start.1) | collective-permute-done | bytes 114720 | tf_op jit(solution)/shard_map/ppermute | solution.py:154
  112.1 14.1 %window.1 = f32[6,128,512]{2,1,0:T(8,128)} custom-call(s32[1]{0:T(128)} %copy.16.selector, f32[6,128,512]{2,1,0:T(8,128)S(1)} %bitcast.16, f32[7,8,512]{2,1,0:T(8,128)S(1)} %collective-permute-done.low, f32[7,8,512]{2,1,0:T(8,128)S(1)} %collective-permute-done.1.high, f32[8,128,512]{2,1,0:T(8,128)S(1)} %copy-done), custom_call_target="tpu_custom_call" | custom-call | tf_op jit(solution)/shard_map/window/pallas_call | solution.py:127
  (8 shorter events, 0.1 us)
Async XLA Ops:
  3.7 7.4 %copy-start.1 = (s32[8]{0:T(128)S(1)}, s32[8]{0:T(128)}, u32[]{:S(2)}) copy-start(s32[8]{0:T(128)} %param.6) | copy-start | bytes 100
  3.7 55.6 %all-to-all-start = ((f32[1,6,128,512]{3,1,0,2:T(8,128)}), f32[1,6,128,512]{3,1,0,2:T(8,128)S(1)}, u32[]{:S(2)}, u32[]{:S(2)}) async-start(f32[1,6,128,512]{3,1,0,2:T(8,128)} %copy.8), calls=%async_computation | async-start | bytes 4194304 | tf_op jit(solution)/shard_map/all_to_all | solution.py:144
  64.8 5.1 %copy-start = (f32[8,128,512]{2,1,0:T(8,128)S(1)}, f32[8,128,512]{2,1,0:T(8,128)}, u32[]{:S(2)}) copy-start(f32[8,128,512]{2,1,0:T(8,128)} %table.1) | copy-start | bytes 6291460
  64.8 41.1 %all-to-all-start.1 = ((f32[8,6,16,512]{3,2,1,0:T(8,128)}), f32[8,6,16,512]{3,2,1,0:T(8,128)}, u32[]{:S(2)}, u32[]{:S(2)}) async-start(f32[8,6,16,512]{3,2,1,0:T(8,128)} %broadcast_select_fusion), calls=%async_computation.1 | async-start | bytes 3145728 | tf_op jit(solution)/shard_map/all_to_all | solution.py:146
  107.6 2.6 %collective-permute-start = (f32[7,8,512]{2,1,0:T(8,128)S(1)}, f32[7,8,512]{2,1,0:T(8,128)S(1)}, u32[]{:S(2)}, u32[]{:S(2)}) collective-permute-start(f32[7,8,512]{2,1,0:T(8,128)S(1)} %get-tuple-element.10), channel_id=1, source_target_pairs={{0,1},{2,3},{4,5},{6,7},{8,9},{10,11},{12,13},{14,15},{16,17},{18,... | collective-permute-start | bytes 344072 | tf_op jit(solution)/shard_map/ppermute | solution.py:153
  108.9 3.2 %collective-permute-start.1 = (f32[7,8,512]{2,1,0:T(8,128)S(1)}, f32[7,8,512]{2,1,0:T(8,128)S(1)}, u32[]{:S(2)}, u32[]{:S(2)}) collective-permute-start(f32[7,8,512]{2,1,0:T(8,128)S(1)} %get-tuple-element.9), channel_id=1, source_target_pairs={{1,0},{3,2},{5,4},{7,6},{9,8},{11,10},{13,12},{15,14},{17,16},{19,... | collective-permute-start | bytes 344072 | tf_op jit(solution)/shard_map/ppermute | solution.py:154

commit v2 on v1

--- a/solution.py
+++ b/solution.py
@@ -139,6 +139,250 @@
         name="window",
     )(selector, parents, low, high, table)
 
+MESH = pl.DeviceIdType.MESH
+PAIR = 2
+HALF = 2 * PAIR
+
+
+def gather_kernel(
+    crossing, picks, places, block, forced, out, low, high, *scratch
+):
+    fields_count, band_rows = block.shape[:2]
+    near, far = scratch[:fields_count], scratch[fields_count : 2 * fields_count]
+    sent_b, sent_c, zeros, a_send, a_recv, b_send, b_recv, c_send, c_recv = scratch[-12:-3]
+    e_send, e_recv, local = scratch[-3:]
+    part = band_rows // PAIR
+    mem, lat = lax.axis_index("mem"), lax.axis_index("lat")
+    half, own = mem // HALF, mem % HALF
+    side = own % PAIR
+    inner_at = (1 - half) * PAIR
+    inner = own // PAIR == 1 - half
+    across = (3 - mem // PAIR) * PAIR + side
+
+    def rows(which):
+        return pl.ds(pl.multiple_of(which * part, HALO), part)
+
+    def remote(src, dst, send, recv, target):
+        return pltpu.make_async_remote_copy(
+            src_ref=src, dst_ref=dst, send_sem=send, recv_sem=recv,
+            device_id=target, device_id_type=MESH,
+        )
+
+    def slot(local_index):
+        return {"mem": half * HALF + local_index}
+
+    def to_inner(f, to, origin):
+        return remote(
+            block.at[f, rows(to)], near[f].at[origin],
+            a_send.at[f, to], a_recv.at[f, origin], slot(inner_at + to),
+        )
+
+    def keep(f):
+        return pltpu.make_async_copy(block.at[f, rows(side)], near[f].at[own], a_recv.at[f, own])
+
+    def over(f):
+        return remote(
+            sent_b.at[f], far[f],
+            b_send.at[f], b_recv.at[f], {"mem": across},
+        )
+
+    def to_slot(f, to, origin):
+        return remote(
+            sent_c.at[f, to], out.at[f, rows(origin)],
+            c_send.at[f, to], c_recv.at[f, origin], slot(to),
+        )
+
+    def stay(f):
+        return pltpu.make_async_copy(sent_c.at[f, own], out.at[f, rows(side)], c_recv.at[f, side])
+
+    barrier = pltpu.get_barrier_semaphore()
+    for step in range(1, HALF):
+        pl.semaphore_signal(
+            barrier, inc=1, device_id=slot((own + step) % HALF), device_id_type=MESH
+        )
+    pl.semaphore_signal(barrier, inc=1, device_id={"mem": across}, device_id_type=MESH)
+    pl.semaphore_signal(barrier, inc=1, device_id={"lat": 1 - lat}, device_id_type=MESH)
+    pl.semaphore_wait(barrier, HALF + 1)
+
+    def send_all(f):
+        for to in range(PAIR):
+            @pl.when(inner & (side == to))
+            def _():
+                keep(f).start()
+
+            @pl.when(jnp.logical_not(inner & (side == to)))
+            def _():
+                to_inner(f, to, own).start()
+
+    for f in range(fields_count):
+        send_all(f)
+
+    def forced_edge(at_lat):
+        first = HALO if at_lat == 0 else 0
+        dst = low if at_lat == 0 else high
+        return remote(
+            forced.at[:, pl.ds(first, HALO)], dst.at[pl.ds(fields_count, 1)],
+            e_send.at[0], e_recv.at[0], {"lat": 1 - lat},
+        )
+
+    def fields_edge(at_lat):
+        first = band_rows - HALO if at_lat == 0 else 0
+        dst = low if at_lat == 0 else high
+        return remote(
+            out.at[:, pl.ds(first, HALO)], dst.at[pl.ds(0, fields_count)],
+            e_send.at[1], e_recv.at[1], {"lat": 1 - lat},
+        )
+
+    def blank(at_lat):
+        return pltpu.make_async_copy(zeros, low if at_lat == 0 else high, local.at[0])
+
+    zeros[...] = jnp.zeros_like(zeros)
+    for at_lat in range(2):
+        @pl.when(lat == at_lat)
+        def _():
+            forced_edge(at_lat).start()
+            blank(at_lat).start()
+
+    def pass_over(f):
+        for origin in range(HALF):
+            @pl.when(own == origin)
+            def _():
+                keep(f).wait()
+
+            @pl.when(own != origin)
+            def _():
+                to_inner(f, 0, origin).wait_recv()
+        for j in range(crossing):
+            sent_b[f, j] = near[f][picks[j]]
+        over(f).start()
+
+    def hand_out(f):
+        over(f).wait_recv()
+        for to in range(HALF):
+            place = places[to]
+            from_near = near[f][jnp.minimum(place, HALF - 1)]
+            from_far = far[f][jnp.maximum(place - HALF, 0)]
+            sent_c[f, to] = jnp.where(place < HALF, from_near, from_far)
+
+            @pl.when(own == to)
+            def _():
+                stay(f).start()
+
+            @pl.when(own != to)
+            def _():
+                to_slot(f, to, side).start()
+
+    @pl.when(inner)
+    def _():
+        pass_over(0)
+        for f in range(1, fields_count):
+            pass_over(f)
+            hand_out(f - 1)
+        hand_out(fields_count - 1)
+
+    def finish(f):
+        for origin in range(PAIR):
+            @pl.when(inner & (side == origin))
+            def _():
+                stay(f).wait()
+
+            @pl.when(jnp.logical_not(inner & (side == origin)))
+            def _():
+                to_slot(f, 0, origin).wait_recv()
+
+    for f in range(fields_count):
+        finish(f)
+    for at_lat in range(2):
+        @pl.when(lat == at_lat)
+        def _():
+            fields_edge(at_lat).start()
+
+    def drain(f):
+        for to in range(PAIR):
+            @pl.when(jnp.logical_not(inner & (side == to)))
+            def _():
+                to_inner(f, to, own).wait_send()
+
+        @pl.when(inner)
+        def _():
+            over(f).wait_send()
+            for to in range(HALF):
+                @pl.when(own != to)
+                def _():
+                    to_slot(f, to, side).wait_send()
+
+    for f in range(fields_count):
+        drain(f)
+    for at_lat in range(2):
+        @pl.when(lat == at_lat)
+        def _():
+            blank(at_lat).wait()
+            for edge in (forced_edge, fields_edge):
+                edge(at_lat).wait_send()
+                edge(1 - at_lat).wait_recv()
+
+
+def gather_parents(crossing, picks, places, block, forced):
+    fields_count, band_rows, columns = block.shape
+    part = band_rows // PAIR
+    edge = jax.ShapeDtypeStruct((fields_count + 1, HALO, columns), jnp.float32)
+    return pl.pallas_call(
+        functools.partial(gather_kernel, crossing),
+        out_shape=[jax.ShapeDtypeStruct(block.shape, jnp.float32), edge, edge],
+        in_specs=[pl.BlockSpec(memory_space=pltpu.SMEM)] * 2 + [pl.BlockSpec(memory_space=pl.ANY)] * 2,
+        out_specs=[pl.BlockSpec(memory_space=pl.ANY)] * 3,
+        scratch_shapes=[
+            *[pltpu.VMEM((HALF, part, columns), jnp.float32)] * fields_count,
+            *[pltpu.VMEM((crossing, part, columns), jnp.float32)] * fields_count,
+            pltpu.VMEM((fields_count, crossing, part, columns), jnp.float32),
+            pltpu.VMEM((fields_count, HALF, part, columns), jnp.float32),
+            pltpu.VMEM((fields_count + 1, HALO, columns), jnp.float32),
+            pltpu.SemaphoreType.DMA((fields_count, PAIR)),
+            pltpu.SemaphoreType.DMA((fields_count, HALF)),
+            pltpu.SemaphoreType.DMA((fields_count,)),
+            pltpu.SemaphoreType.DMA((fields_count,)),
+            pltpu.SemaphoreType.DMA((fields_count, HALF)),
+            pltpu.SemaphoreType.DMA((fields_count, PAIR)),
+            pltpu.SemaphoreType.DMA((2,)),
+            pltpu.SemaphoreType.DMA((2,)),
+            pltpu.SemaphoreType.DMA((1,)),
+        ],
+        compiler_params=pltpu.CompilerParams(
+            collective_id=crossing, has_side_effects=True, vmem_limit_bytes=24 * 1024 * 1024
+        ),
+        name="gather_parents",
+    )(picks, places, block, forced)
+
+
+def gather_by_halves(block, forced, ancestors):
+    half = lax.axis_index("mem") // HALF
+    members = jnp.arange(HALF, dtype=jnp.int32)
+    by_half = ancestors.reshape(2, HALF)
+    other = (1 - jnp.arange(2, dtype=jnp.int32))[:, None] * HALF + members
+    named = jnp.any(by_half[:, :, None] == other[:, None, :], axis=1)
+    rank = jnp.sum(named[:, None, :] & (members[None, :] < members[:, None])[None], axis=2)
+    counts = jnp.max(jnp.sum(named.astype(jnp.int32), axis=1))
+    most = counts
+    groups = lax.axis_size("groups")
+    for step in range(1, groups):
+        moved = lax.ppermute(counts, "groups", [(i, (i + step) % groups) for i in range(groups)])
+        most = jnp.maximum(most, moved)
+    going = lax.dynamic_index_in_dim(named, 1 - half, 0, keepdims=False)
+    going_rank = lax.dynamic_index_in_dim(rank, 1 - half, 0, keepdims=False)
+    coming_rank = lax.dynamic_index_in_dim(rank, half, 0, keepdims=False)
+    picks = jnp.sum(
+        jnp.where(going[None] & (going_rank[None] == members[:, None]), members[None], 0), axis=1
+    ).astype(jnp.int32)
+    parent = lax.dynamic_index_in_dim(by_half, half, 0, keepdims=False)
+    arrived = HALF + jnp.sum(jnp.where(parent[:, None] % HALF == members, coming_rank, 0), axis=1)
+    places = jnp.where(parent // HALF == half, parent % HALF, arrived).astype(jnp.int32)
+    few = HALF // 2
+
+    def run(crossing):
+        return lambda: gather_parents(crossing, picks, places, block, forced)
+
+    return lax.cond(most <= few, run(few), run(HALF))
+
 
 def copy_members(block, ancestors):
     pieces = lax.all_to_all(block, "mem", split_axis=2, concat_axis=0, tiled=True)
@@ -156,11 +400,15 @@
 
 
 def on_device(ensemble, forcing_table, ancestors, selector):
-    parents = copy_members(ensemble, ancestors)
     table_edges = jnp.concatenate([forcing_table[:, :HALO], forcing_table[:, -HALO:]], axis=1)
     chosen = lax.dynamic_index_in_dim(table_edges, selector[0], 0)
-    ends = jnp.concatenate([parents[:, :HALO], parents[:, -HALO:]], axis=1)
-    low, high = edge_rows(jnp.concatenate([ends, chosen], axis=0))
+    by_halves = lax.axis_size("mem") == 2 * HALF and lax.axis_size("lat") == 2
+    if by_halves and ensemble.shape[2] % (PAIR * HALO) == 0:
+        parents, low, high = gather_by_halves(ensemble[0], chosen, ancestors)
+    else:
+        parents = copy_members(ensemble, ancestors)
+        ends = jnp.concatenate([parents[:, :HALO], parents[:, -HALO:]], axis=1)
+        low, high = edge_rows(jnp.concatenate([ends, chosen], axis=0))
     return run_window(parents, low, high, forcing_table, selector, lax.axis_size("lat"))[None]
 
 

time: 127 us -> 110 us (0.87)
  Pallas kernels: 14.1 us -> 102 us
  waiting for transfers between devices: 86 us -> 0.01 us
  starting transfers between devices: 14.4 us -> 2.97 us
  local copies, waits for them, and re-layouts: 9.45 us -> 1.75 us
  between operations: 0.78 us -> 2.09 us
    pallas_call x0 -> x1, Pallas kernels: none -> 86.3 us  [gather_parents(): pl.pallas_call(functools.partial(gather_kernel, crossing), out_shape=[jax...]
    all_to_all x2 -> x0, waiting for transfers between devices: 84.1 us -> none  [the longest x1 48.2 us: copy_members(): lax.all_to_all(block, 'mem', split_axis=2, concat_axis=0, tiled=True)]
    all_to_all x2 -> x0, starting transfers between devices: 11.8 us -> none  [the longest x1 7.38 us: copy_members(): lax.all_to_all(block, 'mem', split_axis=2, concat_axis=0, tiled=True)]
    unnamed x5 -> x2, local copies, waits for them, and re-layouts: 3.69 us -> 0.01 us
    all_to_all x2 -> x0, local copies, waits for them, and re-layouts: 3.65 us -> none  [the longest x1 2.04 us: copy_members(): lax.all_to_all(block, 'mem', split_axis=2, concat_axis=0, tiled=True)]
    gather x1 -> x0, local copies, waits for them, and re-layouts: 2.05 us -> none  [copy_members(): taken = jnp.take(pieces, ancestors, axis=0)]
    ppermute x2 -> x1, waiting for transfers between devices: 1.91 us -> 0.01 us  [gather_by_halves(): lax.ppermute(counts, 'groups', [(i, (i + step) % groups) for i in range(g...]
    select_n x2, other arithmetic: 1.4 us -> 0.03 us  [the longest x1 0.02 us: gather_by_halves(): jnp.where(parent // HALF == half, parent % HALF, arrived).astype(jnp.int32)]
  transfers between devices with their start and end apart: 4 -> 1, of which waited for: 3 -> 0; matrix products, arithmetic and copies ran while one was open for 0% -> 1% of each run, Pallas kernels for 0% -> 0%
where the time goes in v2:
time: 110 us
  Pallas kernels  102 us (93%)
  starting transfers between devices  2.97 us (3%)
  between operations  2.09 us (2%)
  local copies, waits for them, and re-layouts  1.75 us (2%)
  other arithmetic  1.3 us (1%)
    pallas_call x1, Pallas kernels, gather_parents(): pl.pallas_call(functools.partial(gather_kernel, crossing), out_shape=[jax...  86.3 us
    pallas_call x1, Pallas kernels, run_window(): pl.pallas_call(functools.partial(window_kernel, lat_count), out_shape=jax...  15.3 us
    ppermute x1, starting transfers between devices, gather_by_halves(): lax.ppermute(counts, 'groups', [(i, (i + step) % groups) for i in range(g...  2.97 us
  transfers between devices with their start and end apart: 1, of which 0 were waited for; matrix products, arithmetic and copies ran while one was open for 1% of the time, Pallas kernels for 0%

profile of v2, /device:TPU:0, one launch (start us, length us, event | category | flops | bytes accessed | tf_op | source)
XLA Modules:
  0.0 109.8 jit_solution(14264829027901601361)
XLA Ops:
  0.0 0.1 iota_add_fusion
  0.1 0.7 eq.25
  0.8 0.1 compare_reduce_fusion
  0.9 0.1 convert_reduce_fusion.1
  1.0 0.6 reduce_max.9
  1.7 3.0 %collective-permute-start = (s32[]{:T(128)}, s32[]{:T(128)}, u32[]{:S(2)}, u32[]{:S(2)}) collective-permute-start(s32[]{:T(128)} %reduce_max.9), channel_id=1, source_target_pairs={{0,16},{16,0},{1,17},{17,1},{2,18},{18,2},{3,19},{19,3},{4,20},{20... | collective-permute-start | bytes 20 | tf_op jit(solution)/shard_map/ppermute | solution.py:368
  5.3 0.1 convert_reduce_fusion
  5.5 0.2 select_reduce_fusion
  5.7 1.0 fusion.5
  6.7 0.0 collective-permute-done
  8.1 0.0 copy-start
  8.1 86.4 %conditional.1 = ((f32[6,128,512]{2,1,0:T(8,128)}, f32[7,8,512]{2,1,0:T(8,128)S(1)}, f32[7,8,512]{2,1,0:T(8,128)S(1)})) conditional(s32[]{:T(128)} %convert_element_type.10, (s32[4]{0:T(128)S(1)}, s32[4]{0:T(128)S(1)}, f32[6,128,512]{2,1,0:T(8,128)}, f32[1,16,512]{2,1,0:T(8,128)S(1)}) %tuple.19, (s32[4]{0:T(128)S(1)}, s32[4]{0:T(128)S(1)}, ...), branch_computations={%region_6.7_spmd, %region_7.8_spmd} | conditional | bytes 8 | solution.py:384
  8.1 86.3 %gather_parents.2 = (f32[6,128,512]{2,1,0:T(8,128)}, f32[7,8,512]{2,1,0:T(8,128)S(1)}, f32[7,8,512]{2,1,0:T(8,128)S(1)}) custom-call(s32[4]{0:T(128)S(1)} %get-tuple-element.21.picks, s32[4]{0:T(128)S(1)} %get-tuple-element.22.places, f32[6,128,512]{2,1,0:T(8,128)} %get-tuple-element.23.block, f32[1,16,512]{2,1,0:T(8,128)S(1)} %get-tuple-element.24.forced), custom_call_target="tpu_custom_call" | custom-call | tf_op jit(solution)/shard_map/cond/branch_0_fun/gather_parents/pallas_call | solution.py:329
  94.4 0.0 copy-done
  94.5 15.3 %window.1 = f32[6,128,512]{2,1,0:T(8,128)} custom-call(s32[1]{0:T(128)} %copy.11.selector, f32[6,128,512]{2,1,0:T(8,128)} %get-tuple-element.32.parents, f32[7,8,512]{2,1,0:T(8,128)S(1)} %get-tuple-element.33.low, f32[7,8,512]{2,1,0:T(8,128)S(1)} %get-tuple-element.34.high, f32[8,128,512]{2,1,0:T(8,128)S(1)} %copy-done), custom_call_target="tpu_custom_call" | custom-call | tf_op jit(solution)/shard_map/window/pallas_call | solution.py:127
  (7 shorter events, 0.1 us)
Async XLA Ops:
  1.7 5.1 %collective-permute-start = (s32[]{:T(128)}, s32[]{:T(128)}, u32[]{:S(2)}, u32[]{:S(2)}) collective-permute-start(s32[]{:T(128)} %reduce_max.9), channel_id=1, source_target_pairs={{0,16},{16,0},{1,17},{17,1},{2,18},{18,2},{3,19},{19,3},{4,20},{20... | collective-permute-start | bytes 20 | tf_op jit(solution)/shard_map/ppermute | solution.py:368
  8.1 86.4 %copy-start = (f32[8,128,512]{2,1,0:T(8,128)S(1)}, f32[8,128,512]{2,1,0:T(8,128)}, u32[]{:S(2)}) copy-start(f32[8,128,512]{2,1,0:T(8,128)} %table.1) | copy-start | bytes 6291460
